TPU v7x, 32 devices: a whole 2x2x4 slice. The times are simulated.
32 devices in a mesh: groups: 2 (over y), rows: 2 (over x), expert: 4 (over z), pair: 2 (over core).
Axes of the slice: x: 2, y: 2, z: 4, core: 2. Of those that a mesh axis runs over, the one named last changes fastest.
Arguments:
- acts: bfloat16 [512, 6144], P(('groups', 'rows', 'expert'), 'pair'), parts along dimension 0, may hold values from -6 to 6
- grads: bfloat16 [512, 2, 16384], P(('groups', 'rows', 'expert'), None, 'pair'), parts along dimension 0, may hold values from -0.1796875 to 0.1796875
- routes: int32 [512, 2], P(('groups', 'rows', 'expert')), parts along dimension 0, may hold values from 0 to 3, all different within a row; in each aligned block of 32 rows (0 to 31, 32 to 63, ...) at most 24 rows name the same one
- seq_ids: int32 [512], P(('groups', 'rows', 'expert')), parts along dimension 0, may hold values from 0 to 3, never falling along the last dimension, each value on 1 to 96 neighbouring positions
- p_in: bfloat16 [4, 2, 3072, 64], P('expert', 'pair', 'rows'), may hold values from -0.078125 to 0.078125
- p_out: bfloat16 [4, 2, 8192, 64], P('expert', 'pair', 'rows'), may hold values from -0.046875 to 0.046875
Outputs:
- features: float32 [8, 4, 4096], P('groups', 'expert', ('rows', 'pair')), parts along dimension 0
There are 2 independent parts, one for each index of `groups`. A program takes and returns all parts, laid end to end along the dimension named above; an argument that names none is the same for every part. Nothing has to cross between parts.
Inputs may be any that keep to these rules, and one draw needn't show every extreme that they name: `routes`: in the rows of one device (aligned blocks of 32 tokens) no expert is named by more than 24 entries, and in every draw some expert is named by exactly 24 entries in some block; a token never names one expert twice. `seq_ids`: never falling along the tokens; every sequence holds 1 to 96 tokens, one exactly that many.
All inputs are finite; a program needn't handle non-finite values.
Results may differ from a plain program's by a relative error of at most 0.0003.
Values may be sent and summed in bfloat16 or wider, within the bound.
A program may use at most 64 MiB of HBM per device.

v0:
```python
import jax
import jax.numpy as jnp
from jax import lax
from jax.sharding import PartitionSpec as P

SEQS = 4


def bucket_entries(routes, n_experts, capacity):
    flat = routes.reshape(-1)
    expert_range = jnp.arange(n_experts, dtype=jnp.int32)
    member = (flat[:, None] == expert_range[None, :]).astype(jnp.int32)
    places = jnp.cumsum(member, axis=0) - 1
    place = jnp.sum(places * member, axis=1)
    slot_range = jnp.arange(capacity, dtype=jnp.int32)
    hits = member[:, :, None] * (place[:, None, None] == slot_range[None, None, :]).astype(
        jnp.int32
    )
    entry_index = jnp.arange(flat.shape[0], dtype=jnp.int32)
    source = jnp.sum(hits * entry_index[:, None, None], axis=0)
    filled = jnp.sum(hits, axis=0)
    return (source, filled)


def per_device(acts, grads, routes, seq_ids, p_in, p_out):
    tok = routes.shape[0]
    top = routes.shape[1]
    half_d = acts.shape[1]
    half_ff = grads.shape[2]
    k_in = p_in.shape[3]
    k_out = p_out.shape[3]
    feat = k_in * k_out
    n_rows = lax.axis_size("rows")
    n_exp = lax.axis_size("expert") * p_in.shape[0]
    capacity = min(tok, 3 * tok // lax.axis_size("expert"))
    d_piece = half_d // n_rows
    f_piece = half_ff // n_rows
    seq_range = jnp.arange(SEQS, dtype=jnp.int32)
    source, filled = bucket_entries(routes, n_exp, capacity)
    token_of = source // top
    keep = filled.astype(jnp.bfloat16)[:, :, None]
    a_buckets = jnp.take(acts, token_of.reshape(-1), axis=0).reshape(n_exp, capacity, half_d) * keep
    g_buckets = (
        jnp.take(grads.reshape(tok * top, half_ff), source.reshape(-1), axis=0).reshape(
            n_exp, capacity, half_ff
        )
        * keep
    )
    labels = jnp.where(
        filled == 1, jnp.take(seq_ids, token_of.reshape(-1)).reshape(n_exp, capacity), -1
    )
    a_parts = a_buckets.reshape(n_exp, capacity, n_rows, d_piece).transpose(2, 0, 1, 3)
    g_parts = g_buckets.reshape(n_exp, capacity, n_rows, f_piece).transpose(2, 0, 1, 3)
    label_parts = jnp.broadcast_to(labels.astype(jnp.bfloat16)[None], (n_rows, n_exp, capacity))
    a_recv, g_recv, label_recv = (
        lax.all_to_all(
            a_parts.reshape(n_rows * n_exp, capacity, d_piece),
            ("rows", "expert"),
            split_axis=0,
            concat_axis=0,
            tiled=True,
        ),
        lax.all_to_all(
            g_parts.reshape(n_rows * n_exp, capacity, f_piece),
            ("rows", "expert"),
            split_axis=0,
            concat_axis=0,
            tiled=True,
        ),
        lax.all_to_all(
            label_parts.reshape(n_rows * n_exp, capacity),
            ("rows", "expert"),
            split_axis=0,
            concat_axis=0,
            tiled=True,
        ),
    )
    slots = n_rows * n_exp * capacity
    a_rows = a_recv.reshape(slots, d_piece)
    g_rows = g_recv.reshape(slots, f_piece)
    slot_labels = label_recv.reshape(slots).astype(jnp.int32)
    u_part = jnp.dot(a_rows, p_in.reshape(d_piece, k_in), preferred_element_type=jnp.float32)
    v_part = jnp.dot(g_rows, p_out.reshape(f_piece, k_out), preferred_element_type=jnp.float32)
    groups = lax.axis_size(("rows", "pair"))
    share = feat // groups
    u_all, v_all = lax.psum((u_part, v_part), ("rows", "pair"))
    columns = lax.axis_index(("rows", "pair")) * share + jnp.arange(share, dtype=jnp.int32)
    u_cols = jnp.take(u_all, columns // k_out, axis=1)
    v_cols = jnp.take(v_all, columns % k_out, axis=1)
    onehot = (slot_labels[None, :] == seq_range[:, None]).astype(jnp.float32)
    block = jnp.dot(onehot, u_cols * v_cols, precision=lax.Precision.HIGHEST)
    return block.reshape(SEQS, 1, share)


def solution(mesh):
    return jax.shard_map(
        per_device,
        mesh=mesh,
        in_specs=(
            P(("groups", "rows", "expert"), "pair"),
            P(("groups", "rows", "expert"), None, "pair"),
            P(("groups", "rows", "expert"), None),
            P(("groups", "rows", "expert")),
            P("expert", "pair", "rows", None),
            P("expert", "pair", "rows", None),
        ),
        out_specs=P("groups", "expert", ("rows", "pair")),
        check_vma=False,
    )
```

profile of v0, /device:TPU:0, one launch (start us, length us, event | category | flops | bytes accessed | tf_op | source)
XLA Modules:
  0.0 132.2 jit_solution(3614667889216256828)
XLA Ops:
  6.5 0.0 copy-start
  6.5 0.0 copy-start.2
  6.5 0.8 copy.22
  7.4 0.1 eq.62
  7.5 0.1 fusion.13
  7.5 0.1 copy.23
  7.6 0.1 reduce_window_sum.11
  7.7 0.2 select_reduce_fusion
  7.9 0.2 multiply_reduce_fusion
  8.1 0.1 reduce_sum.32
  8.3 1.6 %gather_fusion = s32[96]{0:T(128)S(1)} fusion(s32[32]{0:T(128)} %param.11, s32[1024]{0:T(1024)S(1)} %get-tuple-element.16), kind=kCustom, calls=%fused_computation.2 | custom fusion | bytes 1152 | tf_op jit(solution)/shard_map/jit(_take)/gather | solution.py:50
  9.9 0.1 gather.22
  9.9 0.0 copy-done.2
  9.9 0.9 gather_fusion.1
  10.9 0.0 copy-start.3
  10.9 0.4 gather.24
  11.3 1.0 fusion.4
  12.3 7.3 %all-to-all-start.1 = ((bf16[8,24,1536]{2,1,0:T(8,128)(2,1)}), bf16[8,24,1536]{2,1,0:T(8,128)(2,1)S(1)}, u32[]{:S(2)}, u32[]{:S(2)}) async-start(bf16[8,24,1536]{2,1,0:T(8,128)(2,1)} %bitcast.3), calls=%async_computation.1 | async-start | bytes 1179648 | tf_op jit(solution)/shard_map/all_to_all | solution.py:56
  19.5 0.0 copy-done.3
  19.6 0.4 reshape.266
  20.0 2.7 %gather_fusion.2 = bf16[96,8192]{1,0:T(8,128)(2,1)} fusion(bf16[64,8192]{1,0:T(8,128)(2,1)S(1)} %reshape.266, s32[1024]{0:T(1024)S(1)} %get-tuple-element.15), kind=kCustom, calls=%fused_computation.4 | custom fusion | bytes 3146112 | tf_op jit(solution)/shard_map/jit(_take)/gather | solution.py:44
  22.7 2.9 %gather.26 = bf16[4,24,2,4096]{3,2,1,0:T(2,128)(2,1)S(1)} reshape(bf16[96,8192]{1,0:T(8,128)(2,1)} %gather_fusion.2) | data formatting | bytes 3145728 | tf_op jit(solution)/shard_map/jit(_take)/gather | solution.py:44
  25.6 3.0 %fusion = bf16[4,24,2,4096]{3,1,0,2:T(8,128)(2,1)} fusion(bf16[4,24,2,4096]{3,2,1,0:T(2,128)(2,1)S(1)} %gather.26, pred[4,24]{1,0:T(4,128)(4,1)S(1)} %compare_and_fusion.2, bf16[4,24]{1,0:T(4,128)(2,1)S(1)} %get-tuple-element.12), kind=kLoop, calls=%fused_computation.6 | loop fusion | flops 1572864 | bytes 3146016 | tf_op jit(solution)/shard_map/mul | solution.py:44
  28.6 7.8 %all-to-all-done.1 = bf16[8,24,1536]{2,1,0:T(8,128)(2,1)S(1)} async-done(((bf16[8,24,1536]{2,1,0:T(8,128)(2,1)}), bf16[8,24,1536]{2,1,0:T(8,128)(2,1)S(1)}, u32[]{:S(2)}, u32[]{:S(2)}) %all-to-all-start.1) | async-done | bytes 589856 | tf_op jit(solution)/shard_map/all_to_all | solution.py:56
  36.3 0.0 copy-start.4
  36.3 3.7 %all-to-all-start.2 = ((bf16[8,24,4096]{2,1,0:T(8,128)(2,1)}), bf16[8,24,4096]{2,1,0:T(8,128)(2,1)S(1)}, u32[]{:S(2)}, u32[]{:S(2)}) async-start(bf16[8,24,4096]{2,1,0:T(8,128)(2,1)} %bitcast.32), calls=%async_computation.2 | async-start | bytes 3145728 | tf_op jit(solution)/shard_map/all_to_all | solution.py:63
  40.1 0.6 copy.24
  40.7 0.0 copy-done.4
  40.7 0.9 fusion.10
  41.6 35.0 %all-to-all-done.2 = bf16[8,24,4096]{2,1,0:T(8,128)(2,1)S(1)} async-done(((bf16[8,24,4096]{2,1,0:T(8,128)(2,1)}), bf16[8,24,4096]{2,1,0:T(8,128)(2,1)S(1)}, u32[]{:S(2)}, u32[]{:S(2)}) %all-to-all-start.2) | async-done | bytes 1572896 | tf_op jit(solution)/shard_map/all_to_all | solution.py:63
  76.6 3.3 %all-to-all-start = ((bf16[8,1,24]{2,1,0:T(2,128)(2,1)}), bf16[8,1,24]{2,1,0:T(2,128)(2,1)S(1)}, u32[]{:S(2)}, u32[]{:S(2)}) async-start(bf16[8,1,24]{2,1,0:T(2,128)(2,1)} %copy.24), calls=%async_computation | async-start | bytes 8192 | tf_op jit(solution)/shard_map/all_to_all | solution.py:70
  80.0 0.0 all-reduce.3.cloned.1.call-start
  80.0 0.0 copy-done
  80.0 1.3 fusion.5
  81.3 0.0 all-reduce.3.cloned.1.call-update
  81.3 5.0 %all-to-all-done = bf16[8,1,24]{2,1,0:T(2,128)(2,1)S(1)} async-done(((bf16[8,1,24]{2,1,0:T(2,128)(2,1)}), bf16[8,1,24]{2,1,0:T(2,128)(2,1)S(1)}, u32[]{:S(2)}, u32[]{:S(2)}) %all-to-all-start) | async-done | bytes 416 | tf_op jit(solution)/shard_map/all_to_all | solution.py:70
  86.3 0.1 reshape.271
  86.4 29.7 %all-reduce.3.cloned.1.call-done = (f32[192,64]{0,1:T(8,128)}, f32[192,64]{0,1:T(8,128)}) async-done(((f32[192,64]{0,1:T(8,128)}, f32[192,64]{0,1:T(8,128)}), (f32[192,64]{0,1:T(8,128)}, f32[192,64]{0,1:T(8,128)})) %all-reduce.3.cloned.1.call-update) | async-done | bytes 98320 | tf_op jit(solution)/shard_map/psum | solution.py:86
  116.1 0.0 copy-start.1
  116.1 4.3 %gather_fusion.4 = f32[1024,192]{1,0:T(8,128)S(1)} fusion(f32[192,64]{0,1:T(8,128)} %get-tuple-element.8, s32[1024]{0:T(1024)S(1)} %get-tuple-element.19), kind=kCustom, calls=%fused_computation.1.clone | custom fusion | bytes 1576960 | tf_op jit(solution)/shard_map/jit(_take)/gather | solution.py:89
  120.4 0.0 copy-done.1
  120.4 3.5 %gather_fusion.3 = f32[1024,192]{1,0:T(8,128)S(1)} fusion(f32[192,64]{0,1:T(8,128)S(1)} %copy-done.1, s32[1024]{0:T(1024)S(1)} %get-tuple-element.20), kind=kCustom, calls=%fused_computation.clone | custom fusion | bytes 1576960 | tf_op jit(solution)/shard_map/jit(_take)/gather | solution.py:88
  123.9 0.8 convolution_bitcast_fusion
  124.7 0.6 copy.27
  (9 shorter events, 0.1 us)
Async XLA Ops:
  6.5 73.5 %copy-start = (bf16[1,1,4096,64]{2,3,1,0:T(8,128)(2,1)S(1)}, bf16[1,1,4096,64]{2,3,1,0:T(8,128)(2,1)}, u32[]{:S(2)}) copy-start(bf16[1,1,4096,64]{2,3,1,0:T(8,128)(2,1)} %param.13) | copy-start | bytes 1572868
  6.5 3.4 %copy-start.2 = (bf16[32,3072]{1,0:T(8,128)(2,1)S(1)}, bf16[32,3072]{1,0:T(8,128)(2,1)}, u32[]{:S(2)}) copy-start(bf16[32,3072]{1,0:T(8,128)(2,1)} %param.8) | copy-start | bytes 589828
  10.9 8.7 %copy-start.3 = (bf16[32,2,8192]{2,1,0:T(2,128)(2,1)S(1)}, bf16[32,2,8192]{2,1,0:T(2,128)(2,1)}, u32[]{:S(2)}) copy-start(bf16[32,2,8192]{2,1,0:T(2,128)(2,1)} %param.9) | copy-start | bytes 3145732
  12.3 24.0 %all-to-all-start.1 = ((bf16[8,24,1536]{2,1,0:T(8,128)(2,1)}), bf16[8,24,1536]{2,1,0:T(8,128)(2,1)S(1)}, u32[]{:S(2)}, u32[]{:S(2)}) async-start(bf16[8,24,1536]{2,1,0:T(8,128)(2,1)} %bitcast.3), calls=%async_computation.1 | async-start | bytes 1179648 | tf_op jit(solution)/shard_map/all_to_all | solution.py:56
  36.3 4.4 %copy-start.4 = (bf16[1,1,1536,64]{2,3,1,0:T(8,128)(2,1)S(1)}, bf16[1,1,1536,64]{2,3,1,0:T(8,128)(2,1)}, u32[]{:S(2)}) copy-start(bf16[1,1,1536,64]{2,3,1,0:T(8,128)(2,1)} %param.12) | copy-start | bytes 589828
  36.3 40.3 %all-to-all-start.2 = ((bf16[8,24,4096]{2,1,0:T(8,128)(2,1)}), bf16[8,24,4096]{2,1,0:T(8,128)(2,1)S(1)}, u32[]{:S(2)}, u32[]{:S(2)}) async-start(bf16[8,24,4096]{2,1,0:T(8,128)(2,1)} %bitcast.32), calls=%async_computation.2 | async-start | bytes 3145728 | tf_op jit(solution)/shard_map/all_to_all | solution.py:63
  76.6 9.6 %all-to-all-start = ((bf16[8,1,24]{2,1,0:T(2,128)(2,1)}), bf16[8,1,24]{2,1,0:T(2,128)(2,1)S(1)}, u32[]{:S(2)}, u32[]{:S(2)}) async-start(bf16[8,1,24]{2,1,0:T(2,128)(2,1)} %copy.24), calls=%async_computation | async-start | bytes 8192 | tf_op jit(solution)/shard_map/all_to_all | solution.py:70
  80.0 36.1 %all-reduce.3.cloned.1.call-start = ((), (), s32[]{:S(2)}) async-start(), calls=%async_computation.3 | async-start | bytes 262144 | tf_op jit(solution)/shard_map/psum | solution.py:86
  116.1 4.3 %copy-start.1 = (f32[192,64]{0,1:T(8,128)S(1)}, f32[192,64]{0,1:T(8,128)}, u32[]{:S(2)}) copy-start(f32[192,64]{0,1:T(8,128)} %get-tuple-element.9) | copy-start | bytes 147460
Sparse Core Ops, SparseCore 0:
  83.2 32.8 all-reduce.2
where the time goes:
time: 133 us; the launch traced here: 132 us
  waiting for transfers between devices  77.4 us (58%)
  local copies, waits for them, and re-layouts  19.2 us (14%)
  starting transfers between devices  14.3 us (11%)
  between operations  13.6 us (10%)
  other arithmetic  4.63 us (3%)
  matrix products  2.98 us (2%)
    all_to_all x1, waiting for transfers between devices, per_device(): lax.all_to_all(g_parts.reshape(n_rows * n_exp, capacity, f_piece), ('rows...  35 us
    psum x1, waiting for transfers between devices, per_device(): u_all, v_all = lax.psum((u_part, v_part), ('rows', 'pair'))  29.7 us
    all_to_all x1, waiting for transfers between devices, per_device(): lax.all_to_all(a_parts.reshape(n_rows * n_exp, capacity, d_piece), ('rows...  7.76 us
    all_to_all x1, starting transfers between devices, per_device(): lax.all_to_all(a_parts.reshape(n_rows * n_exp, capacity, d_piece), ('rows...  7.25 us
    gather x2, local copies, waits for them, and re-layouts, per_device(): jnp.take(grads.reshape(tok * top, half_ff), source.reshape(-1), axis=0)  5.56 us
    all_to_all x1, waiting for transfers between devices, per_device(): lax.all_to_all(label_parts.reshape(n_rows * n_exp, capacity), ('rows', 'e...  4.98 us
    gather x1, local copies, waits for them, and re-layouts, per_device(): v_cols = jnp.take(v_all, columns % k_out, axis=1)  4.33 us
    all_to_all x1, starting transfers between devices, per_device(): lax.all_to_all(g_parts.reshape(n_rows * n_exp, capacity, f_piece), ('rows...  3.71 us
  transfers between devices with their start and end apart: 4, of which 4 were waited for; matrix products, arithmetic and copies ran while one was open for 9% of the time, Pallas kernels for 0%

commit v1 on v0

v1 whole, which is shorter than its diff:
```python
import functools

import jax
import jax.numpy as jnp
from jax import lax
from jax.experimental import pallas as pl
from jax.experimental.pallas import tpu as pltpu
from jax.sharding import PartitionSpec as P

SEQS = 4
AXES = ("groups", "rows", "expert", "pair")
MESH = pl.DeviceIdType.MESH


def per_device(acts, grads, routes, seq_ids, p_in, p_out):
    tok, top = routes.shape
    half_d, half_ff = acts.shape[1], grads.shape[2]
    k_in, k_out = p_in.shape[3], p_out.shape[3]
    feat = k_in * k_out
    n_rows, n_exp = lax.axis_size("rows"), lax.axis_size("expert")
    capacity = min(tok, 3 * tok // n_exp)
    d_piece, f_piece = half_d // n_rows, half_ff // n_rows
    member = (routes.reshape(-1)[:, None] == jnp.arange(n_exp)[None, :]).astype(jnp.int32)
    before = jnp.tri(tok * top, k=-1, dtype=jnp.bfloat16)
    places = jnp.dot(
        before, member.astype(jnp.bfloat16), preferred_element_type=jnp.float32
    ).astype(jnp.int32)
    hits = (member[:, :, None] == 1) & (places[:, :, None] == jnp.arange(capacity)[None, None, :])
    hits = hits.reshape(tok * top, n_exp * capacity)
    pick = hits.T.astype(jnp.bfloat16)
    pick_tok = pick.reshape(-1, tok, top).sum(axis=2)
    a_b = jnp.dot(pick_tok, acts, preferred_element_type=jnp.float32).astype(jnp.bfloat16)
    g_b = jnp.dot(
        pick, grads.reshape(tok * top, half_ff), preferred_element_type=jnp.float32
    ).astype(jnp.bfloat16)
    entry_seq = jnp.broadcast_to(seq_ids[:, None], (tok, top)).reshape(-1)
    labels = jnp.sum(jnp.where(hits, entry_seq[:, None] + 1, 0), axis=0) - 1
    labels = labels.astype(jnp.bfloat16).reshape(1, n_exp, capacity)

    def swap(block):
        return lax.all_to_all(
            block.reshape((n_rows * n_exp,) + block.shape[2:]), ("rows", "expert"),
            split_axis=0, concat_axis=0, tiled=True,
        )

    a_rows = swap(a_b.reshape(n_exp, capacity, n_rows, d_piece).transpose(2, 0, 1, 3))
    g_rows = swap(g_b.reshape(n_exp, capacity, n_rows, f_piece).transpose(2, 0, 1, 3))
    label_rows = swap(jnp.broadcast_to(labels, (n_rows, n_exp, capacity)))
    slots = n_rows * n_exp * capacity
    slot_labels = label_rows.reshape(slots).astype(jnp.int32)
    u_part = jnp.dot(
        a_rows.reshape(slots, d_piece), p_in.reshape(d_piece, k_in),
        preferred_element_type=jnp.float32,
    )
    v_part = jnp.dot(
        g_rows.reshape(slots, f_piece), p_out.reshape(f_piece, k_out),
        preferred_element_type=jnp.float32,
    )
    u_all, v_all = lax.psum((u_part, v_part), ("rows", "pair"))
    cols = k_in // lax.axis_size(("rows", "pair"))
    u_cols = lax.dynamic_slice_in_dim(
        u_all, lax.axis_index(("rows", "pair")) * cols, cols, axis=1
    )
    onehot = (slot_labels[:, None] == jnp.arange(SEQS)[None, :]).astype(jnp.float32)
    left = (onehot[:, :, None] * u_cols[:, None, :]).reshape(slots, SEQS * cols)
    block = lax.dot_general(
        left, v_all, (((0,), (0,)), ((), ())), precision=lax.Precision.HIGHEST
    )
    return block.reshape(SEQS, 1, cols * k_out)


def exchange_kernel(
    sizes, acts, grads, routes, seq, p_in, p_out, out,
    a_buf, g_buf, r_buf, wi_buf, wo_buf, cnt_buf, p_buf, s1_buf, e_buf, s2_buf, t_buf, f_buf,
    loc_sem, a_ss, a_rs, g_ss, g_rs, r_ss, r_rs, wi_ss, wi_rs, wo_ss, wo_rs, c_ss, c_rs,
    s1_ss, s1_rs, s2_ss, s2_rs,
):
    n_g, n_r, n_e, n_h = sizes
    n_q = n_g * n_r
    n_slab = n_q * n_h
    n_chip = n_r * n_e
    g, x, z, h = (lax.axis_index(name) for name in AXES)
    q = g * n_r + x
    me = q * n_h + h
    chip = x * n_e + z
    tok, da = a_buf.shape[1], a_buf.shape[2]
    ent, df = g_buf.shape[1], g_buf.shape[2]
    top = ent // tok
    part = tok // n_h

    def rcopy(src, dst, ss, rs, dev):
        return pltpu.make_async_remote_copy(
            src_ref=src, dst_ref=dst, send_sem=ss, recv_sem=rs,
            device_id=dev, device_id_type=MESH,
        )

    def span(gg, xx, width):
        return pl.ds(pl.multiple_of((xx * n_g + gg) * width, 128), width)

    slab = []
    for j in range(1, n_q):
        o = lax.rem(q + j, n_q)
        slab.append((o, o // n_r, lax.rem(o, n_r)))

    wcol_i = pl.ds(pl.multiple_of(g * da, 128), da)
    wcol_o = pl.ds(pl.multiple_of(g * df, 128), df)
    local = [
        pltpu.make_async_copy(acts.at[:, span(g, x, da)], a_buf.at[q], loc_sem.at[0]),
        pltpu.make_async_copy(grads.at[:, span(g, x, df)], g_buf.at[q], loc_sem.at[1]),
        pltpu.make_async_copy(p_in.at[:, wcol_i], wi_buf.at[z], loc_sem.at[2]),
        pltpu.make_async_copy(p_out.at[:, wcol_o], wo_buf.at[z], loc_sem.at[3]),
    ]
    for c in local:
        c.start()

    barrier = pltpu.get_barrier_semaphore()
    count = 0
    for j in range(1, n_slab):
        o = lax.rem(me + j, n_slab)
        oq = o // n_h
        pl.semaphore_signal(
            barrier, inc=1, device_id=(oq // n_r, lax.rem(oq, n_r), z, lax.rem(o, n_h)),
            device_id_type=MESH,
        )
        count += 1
    for j in range(1, n_e):
        oz = lax.rem(z + j, n_e)
        for ox in range(n_r):
            for oh in range(n_h):
                pl.semaphore_signal(barrier, inc=1, device_id=(g, ox, oz, oh), device_id_type=MESH)
                count += 1

    eye = lax.broadcasted_iota(jnp.int32, (tok, tok), 0) == lax.broadcasted_iota(
        jnp.int32, (tok, tok), 1
    )
    for k in range(top):
        row = routes[k : k + 1, :].astype(jnp.float32)
        col = jnp.sum(jnp.where(eye, jnp.broadcast_to(row, (tok, tok)), 0.0), axis=1, keepdims=True)
        r_buf[q, k] = jnp.broadcast_to(col, (tok, 128)).astype(jnp.bfloat16)
    upto = (
        jnp.broadcast_to(seq[...], (8, tok)) <= lax.broadcasted_iota(jnp.int32, (8, tok), 0)
    ).astype(jnp.float32)
    cnt_buf[chip] = jnp.broadcast_to(jnp.sum(upto, axis=1, keepdims=True), (8, 128))

    pl.semaphore_wait(barrier, count)

    def wi_copy(src, owner, to, d):
        return rcopy(src, wi_buf.at[owner], wi_ss.at[d, owner], wi_rs.at[owner], (g, x, to, h))

    def wo_copy(src, owner, to, d):
        return rcopy(src, wo_buf.at[owner], wo_ss.at[d, owner], wo_rs.at[owner], (g, x, to, h))

    for d, step, ok in ((0, 1, z < n_e - 1), (1, -1, z > 0)):

        @pl.when(ok)
        def _():
            wi_copy(p_in.at[:, wcol_i], z, z + step, d).start()
            wo_copy(p_out.at[:, wcol_o], z, z + step, d).start()

    sends = []
    for j, (o, og, ox) in enumerate(slab):
        dev = (og, ox, z, h)
        sends.append(rcopy(r_buf.at[q], r_buf.at[q], r_ss.at[j], r_rs.at[q], dev))
        sends.append(rcopy(acts.at[:, span(og, ox, da)], a_buf.at[q], a_ss.at[j], a_rs.at[q], dev))
        sends.append(rcopy(grads.at[:, span(og, ox, df)], g_buf.at[q], g_ss.at[j], g_rs.at[q], dev))
    others = []
    for j in range(1, n_chip):
        o = lax.rem(chip + j, n_chip)
        others.append(o)
        dev = (g, o // n_e, lax.rem(o, n_e), h)
        sends.append(
            rcopy(cnt_buf.at[chip], cnt_buf.at[chip], c_ss.at[j - 1], c_rs.at[chip], dev)
        )
    for c in sends:
        c.start()

    for step in range(1, n_e):
        for d, sign in ((0, 1), (1, -1)):
            owner = z - sign * step

            @pl.when((owner >= 0) & (owner < n_e))
            def _():
                to = z + sign
                inside = (to >= 0) & (to < n_e)
                wi_copy(wi_buf.at[owner], owner, z, d).wait_recv()

                @pl.when(inside)
                def _():
                    wi_copy(wi_buf.at[owner], owner, to, d).start()

                wo_copy(wo_buf.at[owner], owner, z, d).wait_recv()

                @pl.when(inside)
                def _():
                    wo_copy(wo_buf.at[owner], owner, to, d).start()

    for c in local:
        c.wait()
    here = (g, x, z, h)
    for o, og, ox in slab:
        rcopy(r_buf.at[o], r_buf.at[o], r_ss.at[0], r_rs.at[o], here).wait_recv()
        rcopy(a_buf.at[o], a_buf.at[o], a_ss.at[0], a_rs.at[o], here).wait_recv()
        rcopy(g_buf.at[o], g_buf.at[o], g_ss.at[0], g_rs.at[o], here).wait_recv()

    k_in = wi_buf.shape[1]
    nt = (((1,), (1,)), ((), ()))
    u_all = lax.dot_general(
        a_buf[...].reshape(n_q * tok, da), wi_buf[...].reshape(n_e * k_in, da), nt,
        preferred_element_type=jnp.float32,
    )
    v_all = lax.dot_general(
        g_buf[...].reshape(n_q * ent, df), wo_buf[...].reshape(n_e * k_in, df), nt,
        preferred_element_type=jnp.float32,
    )
    lane = lax.broadcasted_iota(jnp.int32, (tok, 128), 1)
    left = lane < 64
    half_of = jnp.where(left, 0.0, 1.0)

    def picked(rows, ids):
        total = jnp.zeros((tok, 128), jnp.float32)
        for c in range(n_e // 2):
            total += jnp.where(ids == half_of + 2.0 * c, rows[:, c * 128 : (c + 1) * 128], 0.0)
        return total + pltpu.roll(total, 64, 1)

    for o in range(n_q):
        for k in range(top):
            ids = r_buf[o, k].astype(jnp.float32)
            u = picked(u_all[o * tok : (o + 1) * tok], ids)
            v = picked(v_all[o * ent + k * tok : o * ent + (k + 1) * tok], ids)
            both = jnp.where(left, u, v)
            for t in range(n_h):
                p_buf[o, t, k] = both[t * part : (t + 1) * part]

    firsts = []
    for j in range(1, n_slab):
        o = lax.rem(me + j, n_slab)
        oq = o // n_h
        oh = lax.rem(o, n_h)
        c = rcopy(
            p_buf.at[oq, oh], s1_buf.at[me], s1_ss.at[j - 1], s1_rs.at[me],
            (oq // n_r, lax.rem(oq, n_r), z, oh),
        )
        c.start()
        firsts.append((o, c))
    total = p_buf[q, h]
    for o, c in firsts:
        rcopy(s1_buf.at[o], s1_buf.at[o], s1_ss.at[0], s1_rs.at[o], here).wait_recv()
        total += s1_buf[o]
    mine = pl.ds(pl.multiple_of(h * part, 16), part)
    ids = [r_buf[q, k, mine].astype(jnp.float32) for k in range(top)]
    for e in range(n_e):
        m = jnp.zeros((part, 128), jnp.float32)
        for k in range(top):
            m += jnp.where(ids[k] == float(e), total[k], 0.0)
        e_buf[e] = m

    spot = chip * n_h + h
    s2_buf[spot] = e_buf[z]
    n_group = n_chip * n_h
    seconds = []
    for j in range(1, n_group):
        o = lax.rem(spot + j, n_group)
        oc = o // n_h
        oz = lax.rem(oc, n_e)
        c = rcopy(
            e_buf.at[oz], s2_buf.at[spot], s2_ss.at[j - 1], s2_rs.at[spot],
            (g, oc // n_e, oz, lax.rem(o, n_h)),
        )
        c.start()
        seconds.append((o, c))
    cum = cnt_buf[chip]
    for o in others:
        rcopy(cnt_buf.at[o], cnt_buf.at[o], c_ss.at[0], c_rs.at[o], here).wait_recv()
        cum += cnt_buf[o]
    for o, c in seconds:
        rcopy(s2_buf.at[o], s2_buf.at[o], s2_ss.at[0], s2_rs.at[o], here).wait_recv()
    rows = n_group * part
    uv = s2_buf[...].reshape(rows, 128)
    t_buf[...] = uv.T
    cols = k_in // (n_r * n_h)
    ut = t_buf[pl.ds(pl.multiple_of((x * n_h + h) * cols, 8), cols), :]
    pos = lax.broadcasted_iota(jnp.int32, (cols, rows), 1).astype(jnp.float32)
    blocks = []
    for s in range(SEQS):
        keep = pos < cum[s : s + 1, 0:1]
        if s:
            keep &= pos >= cum[s - 1 : s, 0:1]
        blocks.append(jnp.where(keep, ut, 0.0))
    f_buf[...] = lax.dot_general(
        jnp.concatenate(blocks, axis=0), uv, (((1,), (0,)), ((), ())),
        precision=lax.Precision.HIGHEST, preferred_element_type=jnp.float32,
    )
    n_out = SEQS * cols // 2
    even = f_buf[pl.ds(0, n_out, stride=2), :]
    odd = f_buf[pl.ds(1, n_out, stride=2), :]
    out[...] = jnp.where(
        lax.broadcasted_iota(jnp.int32, (n_out, 128), 1) < 64, pltpu.roll(even, 64, 1), odd
    )

    for d, sign in ((0, 1), (1, -1)):
        to = z + sign
        for step in range(n_e):
            owner = z - sign * step

            @pl.when((owner >= 0) & (owner < n_e) & (to >= 0) & (to < n_e))
            def _():
                wi_copy(wi_buf.at[owner], owner, to, d).wait_send()
                wo_copy(wo_buf.at[owner], owner, to, d).wait_send()

    for c in sends:
        c.wait_send()
    for _, c in firsts + seconds:
        c.wait_send()


def per_device_fused(sizes, acts, grads, routes, seq_ids, p_in, p_out):
    n_g, n_r, n_e, n_h = sizes
    tok, half_d = acts.shape
    top, half_ff = grads.shape[1], grads.shape[2]
    k_in = p_in.shape[3]
    n_q = n_g * n_r
    da, df = half_d // n_q, half_ff // n_q
    ent = tok * top
    n_slab, n_chip = n_q * n_h, n_r * n_e
    n_group = n_chip * n_h
    part = tok // n_h
    cols = k_in // (n_r * n_h)
    n_out = SEQS * cols // 2
    bf, f32, dma = jnp.bfloat16, jnp.float32, pltpu.SemaphoreType.DMA
    vmem = pl.BlockSpec(memory_space=pltpu.VMEM)
    hbm = pl.BlockSpec(memory_space=pl.ANY)
    features = pl.pallas_call(
        functools.partial(exchange_kernel, sizes),
        out_shape=jax.ShapeDtypeStruct((n_out, 128), f32),
        in_specs=[hbm, hbm, vmem, vmem, hbm, hbm],
        out_specs=vmem,
        scratch_shapes=[
            pltpu.VMEM((n_q, tok, da), bf),
            pltpu.VMEM((n_q, ent, df), bf),
            pltpu.VMEM((n_q, top, tok, 128), bf),
            pltpu.VMEM((n_e, k_in, da), bf),
            pltpu.VMEM((n_e, k_in, df), bf),
            pltpu.VMEM((n_chip, 8, 128), f32),
            pltpu.VMEM((n_q, n_h, top, part, 128), f32),
            pltpu.VMEM((n_slab, top, part, 128), f32),
            pltpu.VMEM((n_e, part, 128), f32),
            pltpu.VMEM((n_group, part, 128), f32),
            pltpu.VMEM((128, n_group * part), f32),
            pltpu.VMEM((SEQS * cols, 128), f32),
            dma((4,)),
            dma((n_q,)), dma((n_q,)), dma((n_q,)), dma((n_q,)), dma((n_q,)), dma((n_q,)),
            dma((2, n_e)), dma((n_e,)), dma((2, n_e)), dma((n_e,)),
            dma((n_chip,)), dma((n_chip,)),
            dma((n_slab,)), dma((n_slab,)),
            dma((n_group,)), dma((n_group,)),
        ],
        compiler_params=pltpu.CompilerParams(
            collective_id=0, has_side_effects=True, vmem_limit_bytes=24 * 1024 * 1024
        ),
    )(
        acts,
        grads.transpose(1, 0, 2).reshape(ent, half_ff),
        routes.T,
        seq_ids.reshape(1, tok),
        p_in.reshape(p_in.shape[2], k_in).T,
        p_out.reshape(p_out.shape[2], k_in).T,
    )
    return features.reshape(SEQS, 1, -1)


def fits(sizes):
    n_g, n_r, n_e, n_h = sizes
    return n_g * n_r <= 4 and n_e % 2 == 0 and n_e <= 4 and n_h == 2


def solution(mesh):
    sizes = tuple(mesh.shape[name] for name in AXES)
    body = functools.partial(per_device_fused, sizes) if fits(sizes) else per_device
    return jax.shard_map(
        body,
        mesh=mesh,
        in_specs=(
            P(("groups", "rows", "expert"), "pair"),
            P(("groups", "rows", "expert"), None, "pair"),
            P(("groups", "rows", "expert"), None),
            P(("groups", "rows", "expert")),
            P("expert", "pair", "rows", None),
            P("expert", "pair", "rows", None),
        ),
        out_specs=P("groups", "expert", ("rows", "pair")),
        check_vma=False,
    )
```

time: 133 us -> 46.4 us (0.35)
  waiting for transfers between devices: 77.4 us -> 0 us
  Pallas kernels: 0 us -> 43 us
  local copies, waits for them, and re-layouts: 19.2 us -> 3.14 us
  starting transfers between devices: 14.3 us -> 0 us
  between operations: 13.6 us -> 0.06 us
  other arithmetic: 4.63 us -> 0 us
  matrix products: 2.98 us -> 0 us
    all_to_all x3 -> x0, waiting for transfers between devices: 47.7 us -> none  [the longest x1 35 us: per_device(): lax.all_to_all(g_parts.reshape(n_rows * n_exp, capacity, f_piece), ('rows...]
    pallas_call x0 -> x1, Pallas kernels: none -> 43 us  [per_device_fused(): pl.pallas_call(functools.partial(exchange_kernel, sizes), out_shape=jax.S...]
    psum x1 -> x0, waiting for transfers between devices: 29.7 us -> none  [per_device(): u_all, v_all = lax.psum((u_part, v_part), ('rows', 'pair'))]
    gather x8 -> x0, local copies, waits for them, and re-layouts: 16.4 us -> none  [the longest x2 5.56 us: per_device(): jnp.take(grads.reshape(tok * top, half_ff), source.reshape(-1), axis=0)]
    all_to_all x3 -> x0, starting transfers between devices: 14.3 us -> none  [the longest x1 7.25 us: per_device(): lax.all_to_all(a_parts.reshape(n_rows * n_exp, capacity, d_piece), ('rows...]
    mul x2 -> x0, other arithmetic: 3.95 us -> none  [the longest x1 3 us: per_device(): jnp.take(grads.reshape(tok * top, half_ff), source.reshape(-1), axis=0)]
    dot_general x3 -> x0, matrix products: 2.98 us -> none  [the longest x1 1.26 us: per_device(): jnp.dot(g_rows, p_out.reshape(f_piece, k_out), preferred_element_type=jnp...]
    transpose x0 -> x1, local copies, waits for them, and re-layouts: none -> 1.88 us  [per_device_fused(): grads.transpose(1, 0, 2).reshape(ent, half_ff)]
  transfers between devices with their start and end apart: 4 -> 0, of which waited for: 4 -> 0; matrix products, arithmetic and copies ran while one was open for 9% -> 0% of each run, Pallas kernels for 0% -> 0%
where the time goes in v1:
time: 46.4 us; the launch traced here: 46.2 us
  Pallas kernels  43 us (93%)
  local copies, waits for them, and re-layouts  3.14 us (7%)
    pallas_call x1, Pallas kernels, per_device_fused(): pl.pallas_call(functools.partial(exchange_kernel, sizes), out_shape=jax.S...  43 us
    transpose x1, local copies, waits for them, and re-layouts, per_device_fused(): grads.transpose(1, 0, 2).reshape(ent, half_ff)  1.88 us
    unnamed x11, local copies, waits for them, and re-layouts  1.26 us

profile of v1, /device:TPU:0, one launch (start us, length us, event | category | flops | bytes accessed | tf_op | source)
XLA Modules:
  0.0 46.2 jit_solution(5654031269265857851)
XLA Ops:
  0.0 0.0 copy-start
  0.0 0.0 copy-start.1
  0.0 0.0 copy-start.2
  0.0 1.9 %copy.7 = bf16[2,32,8192]{2,1,0:T(8,128)(2,1)S(1)} copy(bf16[2,32,8192]{2,0,1:T(2,128)(2,1)} %bitcast.17) | data formatting | bytes 2097152 | tf_op jit(solution)/shard_map/transpose | solution.py:362
  1.9 0.0 copy-start.3
  1.9 0.0 copy-start.4
  1.9 0.0 copy-done
  1.9 0.0 copy-done.1
  1.9 0.0 copy-done.2
  1.9 0.6 %copy-done.3 = s32[32,2]{0,1:T(2,128)S(1)} copy-done((s32[32,2]{0,1:T(2,128)S(1)}, s32[32,2]{0,1:T(2,128)}, u32[]{:S(2)}) %copy-start.3) | copy-done | bytes 280
  2.6 0.0 copy-done.4
  2.6 43.0 %shard_map.64 = f32[32,128]{1,0:T(8,128)S(1)} custom-call(bf16[32,3072]{1,0:T(8,128)(2,1)S(1)} %copy-done.1, bf16[64,8192]{1,0:T(8,128)(2,1)S(1)} %bitcast.11, s32[2,32]{1,0:T(2,128)S(1)} %bitcast.15, s32[1,32]{1,0:T(1,128)S(1)} %bitcast.16, bf16[64,1536]{1,0:T(8,128)(2,1)S(1)} %bitcast.13, bf16[64,4096]{1,0:T(8,128)(2,1)S(1)} %bitcast.12), custom_call_target="tpu_custom_call" | custom-call | tf_op jit(solution)/shard_map/pallas_call | solution.py:332
  45.6 0.6 %copy.10 = f32[4,1,1024]{2,1,0:T(1,128)} copy(f32[4,1,1024]{2,1,0:T(1,128)S(1)} %bitcast.14) | data formatting | bytes 32768
Async XLA Ops:
  0.0 1.9 %copy-start = (bf16[1,1,4096,64]{2,3,1,0:T(8,128)(2,1)S(1)}, bf16[1,1,4096,64]{2,3,1,0:T(8,128)(2,1)}, u32[]{:S(2)}) copy-start(bf16[1,1,4096,64]{2,3,1,0:T(8,128)(2,1)} %param.11) | copy-start | bytes 1572868
  0.0 1.9 %copy-start.1 = (bf16[32,3072]{1,0:T(8,128)(2,1)S(1)}, bf16[32,3072]{1,0:T(8,128)(2,1)}, u32[]{:S(2)}) copy-start(bf16[32,3072]{1,0:T(8,128)(2,1)} %acts.1) | copy-start | bytes 589828
  0.0 1.9 %copy-start.2 = (bf16[1,1,1536,64]{2,3,1,0:T(8,128)(2,1)S(1)}, bf16[1,1,1536,64]{2,3,1,0:T(8,128)(2,1)}, u32[]{:S(2)}) copy-start(bf16[1,1,1536,64]{2,3,1,0:T(8,128)(2,1)} %param.10) | copy-start | bytes 589828
  1.9 0.7 %copy-start.3 = (s32[32,2]{0,1:T(2,128)S(1)}, s32[32,2]{0,1:T(2,128)}, u32[]{:S(2)}) copy-start(s32[32,2]{0,1:T(2,128)} %param.8) | copy-start | bytes 772
  1.9 0.7 %copy-start.4 = (s32[32]{0:T(128)S(1)}, s32[32]{0:T(128)}, u32[]{:S(2)}) copy-start(s32[32]{0:T(128)} %param.9) | copy-start | bytes 388

commit v2 on v1

--- a/solution.py
+++ b/solution.py
@@ -70,8 +70,8 @@
 
 
 def exchange_kernel(
-    sizes, acts, grads, routes, seq, p_in, p_out, out,
-    a_buf, g_buf, r_buf, wi_buf, wo_buf, cnt_buf, p_buf, s1_buf, e_buf, s2_buf, t_buf, f_buf,
+    sizes, acts, grads, routes_hbm, seq_hbm, p_in, p_out, out,
+    a_buf, g_buf, r_buf, wi_buf, wo_buf, cnt_buf, p_buf, s1_buf, e_buf, s2_buf, t_buf, f_buf, v_buf, g2_buf, routes, seq,
     loc_sem, a_ss, a_rs, g_ss, g_rs, r_ss, r_rs, wi_ss, wi_rs, wo_ss, wo_rs, c_ss, c_rs,
     s1_ss, s1_rs, s2_ss, s2_rs,
 ):
@@ -84,8 +84,8 @@
     me = q * n_h + h
     chip = x * n_e + z
     tok, da = a_buf.shape[1], a_buf.shape[2]
-    ent, df = g_buf.shape[1], g_buf.shape[2]
-    top = ent // tok
+    top, df = g_buf.shape[2], g_buf.shape[3]
+    ent = tok * top
     part = tok // n_h
 
     def rcopy(src, dst, ss, rs, dev):
@@ -106,11 +106,15 @@
     wcol_o = pl.ds(pl.multiple_of(g * df, 128), df)
     local = [
         pltpu.make_async_copy(acts.at[:, span(g, x, da)], a_buf.at[q], loc_sem.at[0]),
-        pltpu.make_async_copy(grads.at[:, span(g, x, df)], g_buf.at[q], loc_sem.at[1]),
+        pltpu.make_async_copy(grads.at[:, :, span(g, x, df)], g_buf.at[q], loc_sem.at[1]),
         pltpu.make_async_copy(p_in.at[:, wcol_i], wi_buf.at[z], loc_sem.at[2]),
         pltpu.make_async_copy(p_out.at[:, wcol_o], wo_buf.at[z], loc_sem.at[3]),
     ]
-    for c in local:
+    small = [
+        pltpu.make_async_copy(routes_hbm, routes, loc_sem.at[4]),
+        pltpu.make_async_copy(seq_hbm, seq, loc_sem.at[5]),
+    ]
+    for c in small + local:
         c.start()
 
     barrier = pltpu.get_barrier_semaphore()
@@ -130,6 +134,8 @@
                 pl.semaphore_signal(barrier, inc=1, device_id=(g, ox, oz, oh), device_id_type=MESH)
                 count += 1
 
+    for c in small:
+        c.wait()
     eye = lax.broadcasted_iota(jnp.int32, (tok, tok), 0) == lax.broadcasted_iota(
         jnp.int32, (tok, tok), 1
     )
@@ -162,7 +168,7 @@
         dev = (og, ox, z, h)
         sends.append(rcopy(r_buf.at[q], r_buf.at[q], r_ss.at[j], r_rs.at[q], dev))
         sends.append(rcopy(acts.at[:, span(og, ox, da)], a_buf.at[q], a_ss.at[j], a_rs.at[q], dev))
-        sends.append(rcopy(grads.at[:, span(og, ox, df)], g_buf.at[q], g_ss.at[j], g_rs.at[q], dev))
+        sends.append(rcopy(grads.at[:, :, span(og, ox, df)], g_buf.at[q], g_ss.at[j], g_rs.at[q], dev))
     others = []
     for j in range(1, n_chip):
         o = lax.rem(chip + j, n_chip)
@@ -194,13 +200,15 @@
                 def _():
                     wo_copy(wo_buf.at[owner], owner, to, d).start()
 
-    for c in local:
-        c.wait()
-    here = (g, x, z, h)
-    for o, og, ox in slab:
-        rcopy(r_buf.at[o], r_buf.at[o], r_ss.at[0], r_rs.at[o], here).wait_recv()
-        rcopy(a_buf.at[o], a_buf.at[o], a_ss.at[0], a_rs.at[o], here).wait_recv()
-        rcopy(g_buf.at[o], g_buf.at[o], g_ss.at[0], g_rs.at[o], here).wait_recv()
+        if step == 1:
+            for c in local:
+                c.wait()
+            here = (g, x, z, h)
+            for o, og, ox in slab:
+                rcopy(r_buf.at[o], r_buf.at[o], r_ss.at[0], r_rs.at[o], here).wait_recv()
+                rcopy(a_buf.at[o], a_buf.at[o], a_ss.at[0], a_rs.at[o], here).wait_recv()
+                rcopy(g_buf.at[o], g_buf.at[o], g_ss.at[0], g_rs.at[o], here).wait_recv()
+            g2_buf[...] = g_buf[...].reshape(n_q * ent, df)
 
     k_in = wi_buf.shape[1]
     nt = (((1,), (1,)), ((), ()))
@@ -209,9 +217,11 @@
         preferred_element_type=jnp.float32,
     )
     v_all = lax.dot_general(
-        g_buf[...].reshape(n_q * ent, df), wo_buf[...].reshape(n_e * k_in, df), nt,
+        g2_buf[...], wo_buf[...].reshape(n_e * k_in, df), nt,
         preferred_element_type=jnp.float32,
     )
+    for c in range(n_e // 2):
+        v_buf[c] = v_all[:, c * 128 : (c + 1) * 128]
     lane = lax.broadcasted_iota(jnp.int32, (tok, 128), 1)
     left = lane < 64
     half_of = jnp.where(left, 0.0, 1.0)
@@ -219,14 +229,14 @@
     def picked(rows, ids):
         total = jnp.zeros((tok, 128), jnp.float32)
         for c in range(n_e // 2):
-            total += jnp.where(ids == half_of + 2.0 * c, rows[:, c * 128 : (c + 1) * 128], 0.0)
+            total += jnp.where(ids == half_of + 2.0 * c, rows[c], 0.0)
         return total + pltpu.roll(total, 64, 1)
 
     for o in range(n_q):
         for k in range(top):
             ids = r_buf[o, k].astype(jnp.float32)
-            u = picked(u_all[o * tok : (o + 1) * tok], ids)
-            v = picked(v_all[o * ent + k * tok : o * ent + (k + 1) * tok], ids)
+            u = picked([u_all[o * tok : (o + 1) * tok, c * 128 : (c + 1) * 128] for c in range(n_e // 2)], ids)
+            v = picked([v_buf[c, pl.ds(o * ent + k, tok, stride=top), :] for c in range(n_e // 2)], ids)
             both = jnp.where(left, u, v)
             for t in range(n_h):
                 p_buf[o, t, k] = both[t * part : (t + 1) * part]
@@ -328,15 +338,15 @@
     n_out = SEQS * cols // 2
     bf, f32, dma = jnp.bfloat16, jnp.float32, pltpu.SemaphoreType.DMA
     vmem = pl.BlockSpec(memory_space=pltpu.VMEM)
-    hbm = pl.BlockSpec(memory_space=pl.ANY)
+    hbm = pl.BlockSpec(memory_space=pltpu.HBM)
     features = pl.pallas_call(
         functools.partial(exchange_kernel, sizes),
         out_shape=jax.ShapeDtypeStruct((n_out, 128), f32),
-        in_specs=[hbm, hbm, vmem, vmem, hbm, hbm],
+        in_specs=[hbm] * 6,
         out_specs=vmem,
         scratch_shapes=[
             pltpu.VMEM((n_q, tok, da), bf),
-            pltpu.VMEM((n_q, ent, df), bf),
+            pltpu.VMEM((n_q, tok, top, df), bf),
             pltpu.VMEM((n_q, top, tok, 128), bf),
             pltpu.VMEM((n_e, k_in, da), bf),
             pltpu.VMEM((n_e, k_in, df), bf),
@@ -347,7 +357,11 @@
             pltpu.VMEM((n_group, part, 128), f32),
             pltpu.VMEM((128, n_group * part), f32),
             pltpu.VMEM((SEQS * cols, 128), f32),
-            dma((4,)),
+            pltpu.VMEM((n_e // 2, n_q * ent, 128), f32),
+            pltpu.VMEM((n_q * ent, df), bf),
+            pltpu.VMEM((top, tok), jnp.int32),
+            pltpu.VMEM((1, tok), jnp.int32),
+            dma((6,)),
             dma((n_q,)), dma((n_q,)), dma((n_q,)), dma((n_q,)), dma((n_q,)), dma((n_q,)),
             dma((2, n_e)), dma((n_e,)), dma((2, n_e)), dma((n_e,)),
             dma((n_chip,)), dma((n_chip,)),
@@ -355,11 +369,11 @@
             dma((n_group,)), dma((n_group,)),
         ],
         compiler_params=pltpu.CompilerParams(
-            collective_id=0, has_side_effects=True, vmem_limit_bytes=24 * 1024 * 1024
+            collective_id=0, has_side_effects=True, vmem_limit_bytes=60 * 1024 * 1024
         ),
     )(
         acts,
-        grads.transpose(1, 0, 2).reshape(ent, half_ff),
+        grads,
         routes.T,
         seq_ids.reshape(1, tok),
         p_in.reshape(p_in.shape[2], k_in).T,

time: 46.4 us -> 45.3 us (0.976)
  local copies, waits for them, and re-layouts: 3.14 us -> 1.32 us
  Pallas kernels: 43 us -> 43.7 us
    transpose x1 -> x0, local copies, waits for them, and re-layouts: 1.88 us -> none  [per_device_fused(): grads.transpose(1, 0, 2).reshape(ent, half_ff)]
    pallas_call x1, Pallas kernels: 43 us -> 43.7 us  [per_device_fused(): pl.pallas_call(functools.partial(exchange_kernel, sizes), out_shape=jax.S...]
    unnamed x11 -> x1, local copies, waits for them, and re-layouts: 1.26 us -> 1.32 us
where the time goes in v2:
time: 45.3 us; the launch traced here: 45 us
  Pallas kernels  43.7 us (96%)
  local copies, waits for them, and re-layouts  1.32 us (3%)
    pallas_call x1, Pallas kernels, per_device_fused(): pl.pallas_call(functools.partial(exchange_kernel, sizes), out_shape=jax.S...  43.7 us
    unnamed x1, local copies, waits for them, and re-layouts  1.32 us

profile of v2, /device:TPU:0, one launch (start us, length us, event | category | flops | bytes accessed | tf_op | source)
XLA Modules:
  0.0 45.0 jit_solution(13740494173477435459)
XLA Ops:
  0.0 43.7 %shard_map.64 = f32[32,128]{1,0:T(8,128)} custom-call(bf16[32,3072]{1,0:T(8,128)(2,1)} %acts.1, bf16[32,2,8192]{2,1,0:T(2,128)(2,1)} %grads.1, s32[2,32]{1,0:T(2,128)} %bitcast.12, s32[1,32]{1,0:T(1,128)} %bitcast.13, bf16[64,1536]{1,0:T(8,128)(2,1)} %bitcast.10, bf16[64,4096]{1,0:T(8,128)(2,1)} %bitcast.9), custom_call_target="tpu_custom_call" | custom-call | tf_op jit(solution)/shard_map/pallas_call | solution.py:342
  43.7 1.3 %copy.9 = f32[4,1,1024]{2,1,0:T(1,128)} copy(f32[4,1,1024]{2,1,0:T(1,128)} %bitcast.11) | data formatting | bytes 32768

commit v3 on v2

--- a/solution.py
+++ b/solution.py
@@ -72,7 +72,9 @@
 def exchange_kernel(
     sizes, acts, grads, routes_hbm, seq_hbm, p_in, p_out, out,
     a_buf, g_buf, r_buf, wi_buf, wo_buf, cnt_buf, p_buf, s1_buf, e_buf, s2_buf, t_buf, f_buf, v_buf, g2_buf, routes, seq,
-    loc_sem, a_ss, a_rs, g_ss, g_rs, r_ss, r_rs, wi_ss, wi_rs, wo_ss, wo_rs, c_ss, c_rs,
+    xa_buf, xg_buf, xr_buf, x_buf, u_buf,
+    loc_sem, a_ss, a_rs, g_ss, g_rs, r_ss, r_rs, w_ss, w_rs, c_ss, c_rs,
+    ae_ss, ae_rs, ge_ss, ge_rs, xa_ss, xa_rs, xg_ss, xg_rs, xr_ss, xr_rs, x_ss,
     s1_ss, s1_rs, s2_ss, s2_rs,
 ):
     n_g, n_r, n_e, n_h = sizes
@@ -94,8 +96,16 @@
             device_id=dev, device_id_type=MESH,
         )
 
-    def span(gg, xx, width):
-        return pl.ds(pl.multiple_of((xx * n_g + gg) * width, 128), width)
+    def span(gg, xx, width, first=0, size=None):
+        start = pl.multiple_of((xx * n_g + gg) * width + first, 128)
+        return pl.ds(start, width if size is None else size)
+
+    ai, gi = xa_buf.shape[2], xg_buf.shape[3]
+    a_main, g_main = pl.ds(ai, da - ai), pl.ds(gi, df - gi)
+    a_lead, g_lead = pl.ds(0, ai), pl.ds(0, gi)
+    at_end = (z == 0) | (z == n_e - 1)
+    low = z * 2 < n_e
+    ally = jnp.where(at_end, jnp.where(low, 1, n_e - 2), jnp.where(low, 0, n_e - 1))
 
     slab = []
     for j in range(1, n_q):
@@ -134,6 +144,15 @@
                 pl.semaphore_signal(barrier, inc=1, device_id=(g, ox, oz, oh), device_id_type=MESH)
                 count += 1
 
+    for j in range(1, n_g):
+        for ox in range(n_r):
+            for oh in range(n_h):
+                pl.semaphore_signal(
+                    barrier, inc=1, device_id=(lax.rem(g + j, n_g), ox, ally, oh),
+                    device_id_type=MESH,
+                )
+                count += 1
+
     for c in small:
         c.wait()
     eye = lax.broadcasted_iota(jnp.int32, (tok, tok), 0) == lax.broadcasted_iota(
@@ -150,25 +169,65 @@
 
     pl.semaphore_wait(barrier, count)
 
-    def wi_copy(src, owner, to, d):
-        return rcopy(src, wi_buf.at[owner], wi_ss.at[d, owner], wi_rs.at[owner], (g, x, to, h))
-
-    def wo_copy(src, owner, to, d):
-        return rcopy(src, wo_buf.at[owner], wo_ss.at[d, owner], wo_rs.at[owner], (g, x, to, h))
-
-    for d, step, ok in ((0, 1, z < n_e - 1), (1, -1, z > 0)):
-
-        @pl.when(ok)
-        def _():
-            wi_copy(p_in.at[:, wcol_i], z, z + step, d).start()
-            wo_copy(p_out.at[:, wcol_o], z, z + step, d).start()
+    kinds = (
+        (p_in, wi_buf, g * da, a_lead, ai), (p_out, wo_buf, g * df, g_lead, gi),
+        (p_in, wi_buf, g * da, a_main, da - ai), (p_out, wo_buf, g * df, g_main, df - gi),
+    )
+
+    def w_copy(kind, owner, to, d, own=False):
+        hbm, buf, first, cols, size = kinds[kind]
+        dst = buf.at[owner, :, cols]
+        src = dst
+        if own:
+            src = hbm.at[:, pl.ds(pl.multiple_of(first + cols.start, 128), size)]
+        return rcopy(src, dst, w_ss.at[kind, d, owner], w_rs.at[kind, owner], (g, x, to, h))
+
+    def takes(kind, to):
+        if kind < 2:
+            return (to > 0) & (to < n_e - 1)
+        return (to >= 0) & (to < n_e)
+
+    ends, inners = [], []
+    for j in range(n_q):
+        o = lax.rem(q + j, n_q)
+        og, ox = o // n_r, lax.rem(o, n_r)
+        dev = (og, ox, ally, h)
+        a_src, g_src = acts.at[:, span(og, ox, da, 0, ai)], grads.at[:, :, span(og, ox, df, 0, gi)]
+        ends.append(rcopy(r_buf.at[q], xr_buf.at[q], xr_ss.at[j], xr_rs.at[q], dev))
+        ends.append(rcopy(a_src, xa_buf.at[q], xa_ss.at[j], xa_rs.at[q], dev))
+        ends.append(rcopy(g_src, xg_buf.at[q], xg_ss.at[j], xg_rs.at[q], dev))
+        if j:
+            dev = (og, ox, z, h)
+            inners.append(
+                rcopy(a_src, a_buf.at[q, :, a_lead], ae_ss.at[j], ae_rs.at[q], dev)
+            )
+            inners.append(
+                rcopy(g_src, g_buf.at[q, :, :, g_lead], ge_ss.at[j], ge_rs.at[q], dev)
+            )
+
+    for kind in range(4):
+        for d, step in ((0, 1), (1, -1)):
+
+            @pl.when(takes(kind, z + step))
+            def _():
+                w_copy(kind, z, z + step, d, own=True).start()
+
+    @pl.when(at_end)
+    def _():
+        for c in ends:
+            c.start()
+
+    @pl.when(jnp.logical_not(at_end))
+    def _():
+        for c in inners:
+            c.start()
 
     sends = []
     for j, (o, og, ox) in enumerate(slab):
         dev = (og, ox, z, h)
         sends.append(rcopy(r_buf.at[q], r_buf.at[q], r_ss.at[j], r_rs.at[q], dev))
-        sends.append(rcopy(acts.at[:, span(og, ox, da)], a_buf.at[q], a_ss.at[j], a_rs.at[q], dev))
-        sends.append(rcopy(grads.at[:, :, span(og, ox, df)], g_buf.at[q], g_ss.at[j], g_rs.at[q], dev))
+        sends.append(rcopy(acts.at[:, span(og, ox, da, ai, da - ai)], a_buf.at[q, :, a_main], a_ss.at[j], a_rs.at[q], dev))
+        sends.append(rcopy(grads.at[:, :, span(og, ox, df, gi, df - gi)], g_buf.at[q, :, :, g_main], g_ss.at[j], g_rs.at[q], dev))
     others = []
     for j in range(1, n_chip):
         o = lax.rem(chip + j, n_chip)
@@ -180,50 +239,24 @@
     for c in sends:
         c.start()
 
-    for step in range(1, n_e):
+    here = (g, x, z, h)
+
+    def pass_on(step, kind_pair):
         for d, sign in ((0, 1), (1, -1)):
             owner = z - sign * step
-
-            @pl.when((owner >= 0) & (owner < n_e))
-            def _():
-                to = z + sign
-                inside = (to >= 0) & (to < n_e)
-                wi_copy(wi_buf.at[owner], owner, z, d).wait_recv()
-
-                @pl.when(inside)
+            for kind in kind_pair:
+
+                @pl.when((owner >= 0) & (owner < n_e) & takes(kind, z))
                 def _():
-                    wi_copy(wi_buf.at[owner], owner, to, d).start()
-
-                wo_copy(wo_buf.at[owner], owner, z, d).wait_recv()
-
-                @pl.when(inside)
-                def _():
-                    wo_copy(wo_buf.at[owner], owner, to, d).start()
-
-        if step == 1:
-            for c in local:
-                c.wait()
-            here = (g, x, z, h)
-            for o, og, ox in slab:
-                rcopy(r_buf.at[o], r_buf.at[o], r_ss.at[0], r_rs.at[o], here).wait_recv()
-                rcopy(a_buf.at[o], a_buf.at[o], a_ss.at[0], a_rs.at[o], here).wait_recv()
-                rcopy(g_buf.at[o], g_buf.at[o], g_ss.at[0], g_rs.at[o], here).wait_recv()
-            g2_buf[...] = g_buf[...].reshape(n_q * ent, df)
+                    w_copy(kind, owner, z, d).wait_recv()
+
+                    @pl.when(takes(kind, z + sign))
+                    def _():
+                        w_copy(kind, owner, z + sign, d).start()
 
     k_in = wi_buf.shape[1]
     nt = (((1,), (1,)), ((), ()))
-    u_all = lax.dot_general(
-        a_buf[...].reshape(n_q * tok, da), wi_buf[...].reshape(n_e * k_in, da), nt,
-        preferred_element_type=jnp.float32,
-    )
-    v_all = lax.dot_general(
-        g2_buf[...], wo_buf[...].reshape(n_e * k_in, df), nt,
-        preferred_element_type=jnp.float32,
-    )
-    for c in range(n_e // 2):
-        v_buf[c] = v_all[:, c * 128 : (c + 1) * 128]
-    lane = lax.broadcasted_iota(jnp.int32, (tok, 128), 1)
-    left = lane < 64
+    left = lax.broadcasted_iota(jnp.int32, (tok, 128), 1) < 64
     half_of = jnp.where(left, 0.0, 1.0)
 
     def picked(rows, ids):
@@ -232,14 +265,88 @@
             total += jnp.where(ids == half_of + 2.0 * c, rows[c], 0.0)
         return total + pltpu.roll(total, 64, 1)
 
-    for o in range(n_q):
-        for k in range(top):
-            ids = r_buf[o, k].astype(jnp.float32)
-            u = picked([u_all[o * tok : (o + 1) * tok, c * 128 : (c + 1) * 128] for c in range(n_e // 2)], ids)
-            v = picked([v_buf[c, pl.ds(o * ent + k, tok, stride=top), :] for c in range(n_e // 2)], ids)
-            both = jnp.where(left, u, v)
-            for t in range(n_h):
-                p_buf[o, t, k] = both[t * part : (t + 1) * part]
+    def project(a_rows, g_rows, w_a, w_g):
+        u = lax.dot_general(
+            a_rows.reshape(n_q * tok, -1), w_a.reshape(n_e * k_in, -1), nt,
+            preferred_element_type=jnp.float32,
+        )
+        v = lax.dot_general(
+            g_rows, w_g.reshape(n_e * k_in, -1), nt, preferred_element_type=jnp.float32
+        )
+        for c in range(n_e // 2):
+            u_buf[c] = u[:, c * 128 : (c + 1) * 128]
+            v_buf[c] = v[:, c * 128 : (c + 1) * 128]
+
+    def choose(ids_ref, dst):
+        for o in range(n_q):
+            for k in range(top):
+                ids = ids_ref[o, k].astype(jnp.float32)
+                u = picked([u_buf[c, o * tok : (o + 1) * tok, :] for c in range(n_e // 2)], ids)
+                v = picked(
+                    [
+                        v_buf[c, pl.ds(o * ent + k, tok, stride=top), :]
+                        for c in range(n_e // 2)
+                    ],
+                    ids,
+                )
+                both = jnp.where(left, u, v)
+                for t in range(n_h):
+                    dst[o, t, k] = both[t * part : (t + 1) * part]
+
+    pass_on(1, (0, 1, 2, 3))
+    pass_on(2, (0, 1, 2, 3))
+    for c in local:
+        c.wait()
+    for o, og, ox in slab:
+        rcopy(r_buf.at[o], r_buf.at[o], r_ss.at[0], r_rs.at[o], here).wait_recv()
+        rows = a_buf.at[o, :, a_main]
+        rcopy(rows, rows, a_ss.at[0], a_rs.at[o], here).wait_recv()
+        rows = g_buf.at[o, :, :, g_main]
+        rcopy(rows, rows, g_ss.at[0], g_rs.at[o], here).wait_recv()
+
+    extras = []
+    for j in range(n_slab):
+        o = lax.rem(me + j, n_slab)
+        oq, oh = o // n_h, lax.rem(o, n_h)
+        extras.append(
+            rcopy(
+                x_buf.at[oq, oh], s1_buf.at[n_slab + me], x_ss.at[j], s1_rs.at[n_slab + me],
+                (oq // n_r, lax.rem(oq, n_r), ally, oh),
+            )
+        )
+
+    @pl.when(jnp.logical_not(at_end))
+    def _():
+        for o in range(n_q):
+            rcopy(xr_buf.at[o], xr_buf.at[o], xr_ss.at[0], xr_rs.at[o], here).wait_recv()
+            rcopy(xa_buf.at[o], xa_buf.at[o], xa_ss.at[0], xa_rs.at[o], here).wait_recv()
+            rcopy(xg_buf.at[o], xg_buf.at[o], xg_ss.at[0], xg_rs.at[o], here).wait_recv()
+        project(
+            xa_buf[...], xg_buf[...].reshape(n_q * ent, gi), wi_buf[:, :, :ai], wo_buf[:, :, :gi]
+        )
+        choose(xr_buf, x_buf)
+        for c in extras:
+            c.start()
+        for o, og, ox in slab:
+            rows = a_buf.at[o, :, a_lead]
+            rcopy(rows, rows, ae_ss.at[0], ae_rs.at[o], here).wait_recv()
+            rows = g_buf.at[o, :, :, g_lead]
+            rcopy(rows, rows, ge_ss.at[0], ge_rs.at[o], here).wait_recv()
+        g2_buf[...] = g_buf[...].reshape(n_q * ent, df)
+        project(a_buf[...], g2_buf[...], wi_buf[...], wo_buf[...])
+
+    @pl.when(at_end)
+    def _():
+        g2_buf[:, gi:] = g_buf[:, :, :, gi:].reshape(n_q * ent, df - gi)
+
+    for step in range(3, n_e):
+        pass_on(step, (2, 3))
+
+    @pl.when(at_end)
+    def _():
+        project(a_buf[:, :, ai:], g2_buf[:, gi:], wi_buf[:, :, ai:], wo_buf[:, :, gi:])
+
+    choose(r_buf, p_buf)
 
     firsts = []
     for j in range(1, n_slab):
@@ -256,6 +363,17 @@
     for o, c in firsts:
         rcopy(s1_buf.at[o], s1_buf.at[o], s1_ss.at[0], s1_rs.at[o], here).wait_recv()
         total += s1_buf[o]
+    p_buf[q, h] = total
+
+    @pl.when(at_end)
+    def _():
+        more = p_buf[q, h]
+        for o in range(n_slab, 2 * n_slab):
+            rcopy(s1_buf.at[o], s1_buf.at[o], s1_ss.at[0], s1_rs.at[o], here).wait_recv()
+            more += s1_buf[o]
+        p_buf[q, h] = more
+
+    total = p_buf[q, h]
     mine = pl.ds(pl.multiple_of(h * part, 16), part)
     ids = [r_buf[q, k, mine].astype(jnp.float32) for k in range(top)]
     for e in range(n_e):
@@ -308,14 +426,29 @@
     )
 
     for d, sign in ((0, 1), (1, -1)):
-        to = z + sign
         for step in range(n_e):
             owner = z - sign * step
-
-            @pl.when((owner >= 0) & (owner < n_e) & (to >= 0) & (to < n_e))
-            def _():
-                wi_copy(wi_buf.at[owner], owner, to, d).wait_send()
-                wo_copy(wo_buf.at[owner], owner, to, d).wait_send()
+            for kind in range(4):
+
+                @pl.when((owner >= 0) & (owner < n_e) & takes(kind, z) & takes(kind, z + sign))
+                def _():
+                    w_copy(kind, owner, z + sign, d).wait_send()
+
+                if step == 0 and kind < 2:
+
+                    @pl.when(at_end & takes(kind, z + sign))
+                    def _():
+                        w_copy(kind, owner, z + sign, d).wait_send()
+
+    @pl.when(at_end)
+    def _():
+        for c in ends:
+            c.wait_send()
+
+    @pl.when(jnp.logical_not(at_end))
+    def _():
+        for c in inners + extras:
+            c.wait_send()
 
     for c in sends:
         c.wait_send()
@@ -330,6 +463,7 @@
     k_in = p_in.shape[3]
     n_q = n_g * n_r
     da, df = half_d // n_q, half_ff // n_q
+    ai, gi = da // 3 // 128 * 128, df * 5 // 16 // 128 * 128
     ent = tok * top
     n_slab, n_chip = n_q * n_h, n_r * n_e
     n_group = n_chip * n_h
@@ -352,7 +486,7 @@
             pltpu.VMEM((n_e, k_in, df), bf),
             pltpu.VMEM((n_chip, 8, 128), f32),
             pltpu.VMEM((n_q, n_h, top, part, 128), f32),
-            pltpu.VMEM((n_slab, top, part, 128), f32),
+            pltpu.VMEM((2 * n_slab, top, part, 128), f32),
             pltpu.VMEM((n_e, part, 128), f32),
             pltpu.VMEM((n_group, part, 128), f32),
             pltpu.VMEM((128, n_group * part), f32),
@@ -361,11 +495,17 @@
             pltpu.VMEM((n_q * ent, df), bf),
             pltpu.VMEM((top, tok), jnp.int32),
             pltpu.VMEM((1, tok), jnp.int32),
+            pltpu.VMEM((n_q, tok, ai), bf),
+            pltpu.VMEM((n_q, tok, top, gi), bf),
+            pltpu.VMEM((n_q, top, tok, 128), bf),
+            pltpu.VMEM((n_q, n_h, top, part, 128), f32),
+            pltpu.VMEM((n_e // 2, n_q * tok, 128), f32),
             dma((6,)),
             dma((n_q,)), dma((n_q,)), dma((n_q,)), dma((n_q,)), dma((n_q,)), dma((n_q,)),
-            dma((2, n_e)), dma((n_e,)), dma((2, n_e)), dma((n_e,)),
+            dma((4, 2, n_e)), dma((4, n_e)),
             dma((n_chip,)), dma((n_chip,)),
-            dma((n_slab,)), dma((n_slab,)),
+            *[dma((n_q,)) for _ in range(10)], dma((n_slab,)),
+            dma((n_slab,)), dma((2 * n_slab,)),
             dma((n_group,)), dma((n_group,)),
         ],
         compiler_params=pltpu.CompilerParams(
@@ -384,7 +524,7 @@
 
 def fits(sizes):
     n_g, n_r, n_e, n_h = sizes
-    return n_g * n_r <= 4 and n_e % 2 == 0 and n_e <= 4 and n_h == 2
+    return n_g * n_r <= 4 and n_e == 4 and n_h == 2
 
 
 def solution(mesh):

time: 45.3 us -> 43.6 us (0.962)
  Pallas kernels: 43.7 us -> 42 us
    pallas_call x1, Pallas kernels: 43.7 us -> 42 us  [per_device_fused(): pl.pallas_call(functools.partial(exchange_kernel, sizes), out_shape=jax.S...]
where the time goes in v3:
time: 43.6 us; the launch traced here: 43.3 us
  Pallas kernels  42 us (96%)
  local copies, waits for them, and re-layouts  1.32 us (3%)
    pallas_call x1, Pallas kernels, per_device_fused(): pl.pallas_call(functools.partial(exchange_kernel, sizes), out_shape=jax.S...  42 us
    unnamed x1, local copies, waits for them, and re-layouts  1.32 us

profile of v3, /device:TPU:0, one launch (start us, length us, event | category | flops | bytes accessed | tf_op | source)
XLA Modules:
  0.0 43.3 jit_solution(13294670066457927165)
XLA Ops:
  0.0 42.0 %shard_map.64 = f32[32,128]{1,0:T(8,128)} custom-call(bf16[32,3072]{1,0:T(8,128)(2,1)} %acts.1, bf16[32,2,8192]{2,1,0:T(2,128)(2,1)} %grads.1, s32[2,32]{1,0:T(2,128)} %bitcast.12, s32[1,32]{1,0:T(1,128)} %bitcast.13, bf16[64,1536]{1,0:T(8,128)(2,1)} %bitcast.10, bf16[64,4096]{1,0:T(8,128)(2,1)} %bitcast.9), custom_call_target="tpu_custom_call" | custom-call | tf_op jit(solution)/shard_map/pallas_call | solution.py:476
  42.0 1.3 %copy.9 = f32[4,1,1024]{2,1,0:T(1,128)} copy(f32[4,1,1024]{2,1,0:T(1,128)} %bitcast.11) | data formatting | bytes 32768
